TPU v7x, 32 devices: a whole 2x2x4 slice. The times are simulated.
32 devices in a mesh: read: 4 (over y, x), row: 8 (over z, core).
Axes of the slice: x: 2, y: 2, z: 4, core: 2. Of those that a mesh axis runs over, the one named last changes fastest.
Arguments:
- snapshots: float32 [256, 40960], P(('read', 'row')), may hold values from -400 to 400
- coefficients: float32 [256, 256], replicated, may hold values from -0.375 to 0.375
Outputs:
- modes: float32 [256, 40960], P(('read', 'row'))
All inputs are finite; a program needn't handle non-finite values.
Results may differ from a plain program's by a relative error of at most 0.000078.
Values sent between devices are 32-bit elements; how exact they have to be, the bound alone decides.
A program may use at most 192 MiB of HBM per device.

v0:
```python
import math

import jax
import jax.numpy as jnp
from jax import lax
from jax.sharding import PartitionSpec as P


def inner_products(left_block, right_block):
    return lax.dot_general(
        left_block,
        right_block,
        (((1,), (1,)), ((), ())),
        precision=lax.Precision.HIGHEST,
        preferred_element_type=jnp.float32,
    )


def lower_cholesky(matrix):
    return jnp.linalg.cholesky(matrix)


def lower_inverse(lower):
    identity = jnp.eye(lower.shape[0], dtype=jnp.float32)
    return lax.linalg.triangular_solve(lower, identity, left_side=True, lower=True)


def shards(snapshots, coefficients):
    count_read = lax.axis_size("read")
    count_row = lax.axis_size("row")
    regrouped = lax.all_to_all(snapshots, ("read", "row"), split_axis=1, concat_axis=0, tiled=True)
    local_rows = regrouped.shape[1]
    total_rows = local_rows * count_read * count_row
    gram_part = inner_products(regrouped, regrouped)
    gram_total = lax.psum(gram_part, ("read", "row"))
    lower_factor = lower_cholesky(gram_total)
    inverse_lower = lower_inverse(lower_factor)
    row_scale = math.sqrt(total_rows)
    basis_rows = jnp.dot(
        inverse_lower,
        regrouped,
        precision=lax.Precision.HIGHEST,
        preferred_element_type=jnp.float32,
    )
    mode_part = row_scale * jnp.dot(
        coefficients.T,
        basis_rows,
        precision=lax.Precision.HIGHEST,
        preferred_element_type=jnp.float32,
    )
    modes = lax.all_to_all(mode_part, ("read", "row"), split_axis=0, concat_axis=1, tiled=True)
    return modes


def solution(mesh):
    in_specs = (P(("read", "row"), None), P())
    out_specs = P(("read", "row"), None)
    return jax.shard_map(shards, mesh=mesh, in_specs=in_specs, out_specs=out_specs, check_vma=False)
```

profile of v0, /device:TPU:0, one launch (start us, length us, event | category | flops | bytes accessed | tf_op | source)
XLA Modules:
  0.0 281.9 jit_solution(5188131096908206286)
XLA Ops:
  6.5 40.5 %all_to_all.38 = f32[8,32,1280]{2,0,1:T(8,128)S(1)} all-to-all(f32[8,32,1280]{2,0,1:T(8,128)} %bitcast.49), channel_id=1, replica_groups=mesh['read'=4,'row'=8] {'read','row'}, dimensions={1} | all-to-all | bytes 2621440 | tf_op jit(solution)/shard_map/all_to_all | solution.py:31
  47.1 1.9 fusion.3
  49.1 122.8 %all-reduce.3.cloned.1.call-done = f32[256,256]{0,1:T(8,128)} async-done(((f32[256,256]{0,1:T(8,128)}), f32[256,256]{0,1:T(8,128)}) %all-reduce.3.cloned.1.call-update) | async-done | bytes 262160 | tf_op jit(solution)/shard_map/psum | solution.py:35
  171.8 1.1 copy.4
  172.9 1.0 fusion.8
  173.9 11.7 %cholesky.50 = f32[128,128]{1,0:T(8,128)S(1)} custom-call(f32[128,128]{1,0:T(8,128)S(1)} %cholesky.118), custom_call_target="Cholesky" | custom-call | tf_op jit(solution)/shard_map/jit(cholesky)/cholesky | solution.py:20
  185.7 9.8 %custom-call.14 = f32[1,128,128]{1,2,0:T(8,128)S(1)} custom-call(f32[1,128,128]{2,1,0:T(8,128)S(1)} %get-tuple-element.26), custom_call_target="InvertDiagBlocksLowerTriangular" | custom-call | tf_op jit(solution)/shard_map/jit(cholesky)/cholesky | solution.py:20
  195.5 0.2 constant_dynamic-update-slice_fusion.1
  195.7 0.3 convolution_subtract_fusion.1
  196.0 11.7 %cholesky.105 = f32[128,128]{1,0:T(8,128)S(1)} custom-call(f32[128,128]{1,0:T(8,128)S(1)} %convolution_subtract_fusion.1), custom_call_target="Cholesky" | custom-call | tf_op jit(solution)/shard_map/jit(cholesky)/cholesky | solution.py:20
  207.8 0.7 compare_reduce_fusion
  209.9 4.1 %while.1 = (s32[]{:T(128)}, f32[256,256]{1,0:T(8,128)S(1)}, s32[2,2]{1,0:T(2,128)S(1)}, f32[2,128,128]{2,1,0:T(8,128)S(1)}, s32[]{:T(128)}) while((s32[]{:T(128)}, f32[256,256]{1,0:T(8,128)S(1)}, s32[2,2]{1,0:T(2,128)S(1)}, f32[2,128,128]{2,1,0:T(8,128)S(1)}, s32[]{:T(128)}) %tuple.23), condition=%wide.while_cond, body=%wide.while_body.sunk | while | flops 2 | bytes 131189 | solution.py:25
  209.9 0.6 fusion.25
  210.5 1.4 bitcast_dynamic-update-slice_fusion.2
  212.0 0.6 fusion.25
  212.6 1.4 bitcast_dynamic-update-slice_fusion.2
  214.0 19.9 %custom-call.15 = f32[2,128,128]{1,2,0:T(8,128)S(1)} custom-call(f32[2,128,128]{2,1,0:T(8,128)S(1)} %get-tuple-element.12), custom_call_target="InvertDiagBlocksLowerTriangular" | custom-call | tf_op jit(solution)/shard_map/triangular_solve | solution.py:25
  233.9 0.3 fusion.9
  234.2 0.3 convolution_subtract_fusion
  234.4 0.3 fusion.12
  234.7 1.2 fusion.1
  236.0 1.3 fusion
  237.3 36.6 %all_to_all.39 = f32[32,8,1280]{2,1,0:T(8,128)S(1)} all-to-all(f32[32,8,1280]{2,1,0:T(8,128)S(1)} %fusion), channel_id=1, replica_groups=mesh['read'=4,'row'=8] {'read','row'}, dimensions={0} | all-to-all | bytes 2621440 | tf_op jit(solution)/shard_map/all_to_all | solution.py:51
  274.0 1.1 copy.20
  (15 shorter events, 0.3 us)
Async XLA Ops:
  6.5 229.5 %copy-start = (f32[256,256]{1,0:T(8,128)S(1)}, f32[256,256]{1,0:T(8,128)}, u32[]{:S(2)}) copy-start(f32[256,256]{1,0:T(8,128)} %param.3) | copy-start | bytes 786436
  6.5 165.3 %all-reduce.3.cloned.1.call-start = ((), (), s32[]{:S(2)}) async-start(), calls=%async_computation.2 | async-start | bytes 524288 | tf_op jit(solution)/shard_map/psum | solution.py:35
Sparse Core Ops, SparseCore 0:
  49.1 122.6 all-reduce.2
where the time goes:
time: 282 us
  waiting for transfers between devices  123 us (44%)
  blocking collectives  77.1 us (27%)
  other arithmetic  54.9 us (19%)
  between operations  14.9 us (5%)
  local copies, waits for them, and re-layouts  6.29 us (2%)
  matrix products  5.82 us (2%)
    psum x1, waiting for transfers between devices, shards(): gram_total = lax.psum(gram_part, ('read', 'row'))  123 us
    all_to_all x1, blocking collectives, shards(): lax.all_to_all(snapshots, ('read', 'row'), split_axis=1, concat_axis=0, t...  40.5 us
    all_to_all x1, blocking collectives, shards(): lax.all_to_all(mode_part, ('read', 'row'), split_axis=0, concat_axis=1, t...  36.6 us
    another operation x6, other arithmetic, lower_cholesky(): return jnp.linalg.cholesky(matrix)  34 us
    another operation x3, other arithmetic, lower_inverse(): lax.linalg.triangular_solve(lower, identity, left_side=True, lower=True)  19.9 us
  transfers between devices with their start and end apart: 1, of which 1 were waited for; matrix products, arithmetic and copies ran while one was open for 0% of the time, Pallas kernels for 0%

commit v1 on v0

v1 whole, which is shorter than its diff:
```python
import functools
import math

import jax
import jax.numpy as jnp
from jax import lax
from jax.experimental import pallas as pl
from jax.experimental.pallas import tpu as pltpu
from jax.sharding import PartitionSpec as P

AXES = ("read", "row")
HIGHEST = lax.Precision.HIGHEST
NN = (((1,), (0,)), ((), ()))
NT = (((1,), (1,)), ((), ()))
VMEM_BYTES = 48 * 1024 * 1024


def product(left, right, dims=NN):
    return lax.dot_general(left, right, dims, precision=HIGHEST, preferred_element_type=jnp.float32)


def position(count_row):
    return lax.axis_index("read") * count_row + lax.axis_index("row")


def coordinates(index, count_row):
    return (lax.div(index, count_row), lax.rem(index, count_row))


def greet(count, count_row, me):
    barrier = pltpu.get_barrier_semaphore()

    def signal(offset, carry):
        other = lax.rem(me + offset, count)
        pl.semaphore_signal(
            barrier, inc=1, device_id=coordinates(other, count_row), device_id_type=pl.DeviceIdType.MESH
        )
        return carry

    lax.fori_loop(1, count, signal, 0)
    return barrier


def wait_bytes(ref, semaphore):
    pltpu.make_async_copy(ref, ref, semaphore).wait()


def gram_kernel(count, count_row, chunks, snap_ref, gram_ref, held_ref, part, slabs,
                local_sem, send_sem, recv_sem):
    me = position(count_row)
    share = snap_ref.shape[0]
    width = held_ref.shape[1]
    piece = width // chunks
    others = (count - 1) * share
    barrier = greet(count, count_row, me)
    mine = pl.ds(pl.multiple_of(me * share, share), share)
    own = pltpu.make_async_copy(
        snap_ref.at[:, pl.ds(pl.multiple_of(me * width, width), width)], held_ref.at[mine, :], local_sem
    )
    own.start()
    pl.semaphore_wait(barrier, count - 1)

    def send(source, target, other, stage):
        pltpu.make_async_remote_copy(
            src_ref=source,
            dst_ref=target,
            send_sem=send_sem.at[stage],
            recv_sem=recv_sem.at[stage],
            device_id=coordinates(other, count_row),
            device_id_type=pl.DeviceIdType.MESH,
        ).start()

    for chunk in range(chunks):
        def scatter(offset, carry, chunk=chunk):
            other = lax.rem(me + offset, count)
            send(
                snap_ref.at[:, pl.ds(pl.multiple_of(other * width + chunk * piece, 128), piece)],
                held_ref.at[mine, pl.ds(chunk * piece, piece)],
                other,
                chunk,
            )
            return carry

        lax.fori_loop(1, count, scatter, 0)

    own.wait()
    for chunk in range(chunks):
        columns = pl.ds(chunk * piece, piece)
        wait_bytes(held_ref.at[pl.ds(0, others), columns], recv_sem.at[chunk])
        block = held_ref[:, columns]
        term = product(block, block, NT)
        if chunk:
            part[...] += term
        else:
            part[...] = term

    slabs[pl.ds(me, 1)] = part[mine, :][None]

    def scatter_part(offset, carry):
        other = lax.rem(me + offset, count)
        rows = pl.ds(pl.multiple_of(other * share, share), share)
        send(part.at[rows, :], slabs.at[me], other, chunks)
        return carry

    lax.fori_loop(1, count, scatter_part, 0)
    wait_bytes(part.at[pl.ds(0, others), :], recv_sem.at[chunks])
    gram_ref[mine, :] = jnp.sum(slabs[...], axis=0)

    def share_total(offset, carry):
        other = lax.rem(me + offset, count)
        send(gram_ref.at[mine, :], gram_ref.at[mine, :], other, chunks + 1)
        return carry

    lax.fori_loop(1, count, share_total, 0)
    wait_bytes(part.at[pl.ds(0, others), :], recv_sem.at[chunks + 1])
    for chunk in range(chunks):
        wait_bytes(held_ref.at[pl.ds(0, others), pl.ds(0, piece)], send_sem.at[chunk])
    wait_bytes(part.at[pl.ds(0, others), :], send_sem.at[chunks])
    wait_bytes(part.at[pl.ds(0, others), :], send_sem.at[chunks + 1])


def modes_kernel(count, count_row, groups, fold_ref, held_ref, out_ref, modes, local_sem, send_sem, recv_sem):
    me = position(count_row)
    snaps, width = held_ref.shape
    share = out_ref.shape[0]
    rows = snaps // groups
    dests = rows // share
    barrier = greet(count, count_row, me)
    target = pl.ds(pl.multiple_of(me * width, width), width)
    first = lax.div(me, dests)

    for step in range(groups):
        group = lax.rem(first + step, groups)
        span = pl.ds(pl.multiple_of(group * rows, rows), rows)
        modes[span, :] = product(fold_ref[span, :], held_ref[...])
        if step == 0:
            own = pltpu.make_async_copy(
                modes.at[pl.ds(pl.multiple_of(me * share, share), share), :], out_ref.at[:, target], local_sem
            )
            own.start()
            pl.semaphore_wait(barrier, count - 1)

        def scatter(offset, carry):
            other = group * dests + lax.rem(lax.rem(me, dests) + offset, dests)
            pltpu.make_async_remote_copy(
                src_ref=modes.at[pl.ds(pl.multiple_of(other * share, share), share), :],
                dst_ref=out_ref.at[:, target],
                send_sem=send_sem,
                recv_sem=recv_sem,
                device_id=coordinates(other, count_row),
                device_id_type=pl.DeviceIdType.MESH,
            ).start()
            return carry

        lax.fori_loop(1 if step == 0 else 0, dests, scatter, 0)

    others = modes.at[pl.ds(0, (count - 1) * share), :]
    own.wait()
    wait_bytes(others, recv_sem)
    wait_bytes(others, send_sem)


def eliminate(block):
    size = block.shape[0]
    row_id = lax.broadcasted_iota(jnp.int32, (size, 2 * size), 0)
    col_id = lax.broadcasted_iota(jnp.int32, (size, 2 * size), 1)
    state = jnp.concatenate([block, jnp.zeros_like(block)], axis=1)
    state = jnp.where(col_id == row_id + size, 1.0, state)
    for k in range(size - 1):
        pivot_row = state[k : k + 1, :]
        inverse = 1.0 / state[k : k + 1, k : k + 1]
        scaled = pivot_row * inverse
        low = (k + 1) // 8 * 8
        below = state[low:, :]
        column = below[:, k : k + 1]
        if low <= k:
            column = jnp.where(row_id[low:, :1] > k, column, 0.0)
        below = below - column * scaled
        state = jnp.concatenate([state[:low], below], axis=0) if low else below
    pivots = jnp.sum(jnp.where(col_id == row_id, state, 0.0), axis=1, keepdims=True)
    return state[:, size:] * lax.rsqrt(pivots)


def factor_kernel(size, scale, gram_ref, coef_ref, fold_ref, work, inverse):
    total = gram_ref.shape[0]
    blocks = total // size
    work[...] = gram_ref[...]
    inverse[...] = jnp.zeros_like(inverse)
    for k in range(blocks):
        here = slice(k * size, (k + 1) * size)
        low = eliminate(work[here, here])
        before = slice(0, k * size)
        after = slice((k + 1) * size, total)
        if k:
            inverse[here, before] = product(low, inverse[here, before])
        inverse[here, here] = low
        if k < blocks - 1:
            across = product(low, work[here, after])
            down = product(work[after, here], low, NT)
            work[after, after] -= product(down, across)
            inverse[after, slice(0, (k + 1) * size)] -= product(down, inverse[here, slice(0, (k + 1) * size)])
    fold_ref[...] = scale * lax.dot_general(
        coef_ref[...], inverse[...], (((0,), (0,)), ((), ())),
        precision=HIGHEST, preferred_element_type=jnp.float32,
    )


def vmem_spec():
    return pl.BlockSpec(memory_space=pltpu.VMEM)


def any_spec():
    return pl.BlockSpec(memory_space=pl.ANY)


def cost(flops, moved):
    return pl.CostEstimate(flops=flops, bytes_accessed=moved, transcendentals=0)


def factor(gram, coefficients, scale):
    snaps = gram.shape[0]
    return pl.pallas_call(
        functools.partial(factor_kernel, 64, scale),
        out_shape=jax.ShapeDtypeStruct((coefficients.shape[1], snaps), jnp.float32),
        in_specs=[vmem_spec()] * 2,
        out_specs=vmem_spec(),
        scratch_shapes=[pltpu.VMEM((snaps, snaps), jnp.float32)] * 2,
        compiler_params=pltpu.CompilerParams(vmem_limit_bytes=VMEM_BYTES),
        cost_estimate=cost(6 * snaps**3, 12 * snaps**2),
        name="factor",
    )(gram, coefficients)


def direct(snapshots, coefficients, count, count_row):
    share, total_rows = snapshots.shape
    snaps, width = share * count, total_rows // count
    chunks = 2 if width % 256 == 0 else 1
    gram, held = pl.pallas_call(
        functools.partial(gram_kernel, count, count_row, chunks),
        out_shape=(
            jax.ShapeDtypeStruct((snaps, snaps), jnp.float32),
            jax.ShapeDtypeStruct((snaps, width), jnp.float32),
        ),
        in_specs=[any_spec()],
        out_specs=(vmem_spec(), vmem_spec()),
        scratch_shapes=[
            pltpu.VMEM((snaps, snaps), jnp.float32),
            pltpu.VMEM((count, share, snaps), jnp.float32),
            pltpu.SemaphoreType.DMA,
            pltpu.SemaphoreType.DMA((chunks + 2,)),
            pltpu.SemaphoreType.DMA((chunks + 2,)),
        ],
        compiler_params=pltpu.CompilerParams(
            collective_id=0, has_side_effects=True, vmem_limit_bytes=VMEM_BYTES
        ),
        cost_estimate=cost(2 * snaps * snaps * width, 8 * snaps * width),
        name="gram",
    )(snapshots)
    folded = factor(gram, coefficients, math.sqrt(total_rows))
    return pl.pallas_call(
        functools.partial(modes_kernel, count, count_row, 4),
        out_shape=jax.ShapeDtypeStruct((share, total_rows), jnp.float32),
        in_specs=[vmem_spec(), vmem_spec()],
        out_specs=any_spec(),
        scratch_shapes=[
            pltpu.VMEM((snaps, width), jnp.float32),
            pltpu.SemaphoreType.DMA,
            pltpu.SemaphoreType.DMA,
            pltpu.SemaphoreType.DMA,
        ],
        compiler_params=pltpu.CompilerParams(
            collective_id=1, has_side_effects=True, vmem_limit_bytes=VMEM_BYTES
        ),
        cost_estimate=cost(2 * snaps * snaps * width, 8 * snaps * width),
        name="modes",
    )(folded, held)


def shards(snapshots, coefficients):
    count_row = lax.axis_size("row")
    count = lax.axis_size("read") * count_row
    if snapshots.shape[0] % 8 == 0 and count % 4 == 0:
        return direct(snapshots, coefficients, count, count_row)
    held = lax.all_to_all(snapshots, AXES, split_axis=1, concat_axis=0, tiled=True)
    gram = lax.psum(product(held, held, NT), AXES)
    folded = factor(gram, coefficients, math.sqrt(snapshots.shape[1]))
    return lax.all_to_all(product(folded, held), AXES, split_axis=0, concat_axis=1, tiled=True)


def solution(mesh):
    in_specs = (P(AXES, None), P())
    out_specs = P(AXES, None)
    return jax.shard_map(shards, mesh=mesh, in_specs=in_specs, out_specs=out_specs, check_vma=False)
```

time: 282 us -> 112 us (0.40)
  waiting for transfers between devices: 123 us -> 0 us
  Pallas kernels: 0 us -> 109 us
  blocking collectives: 77.1 us -> 0 us
  other arithmetic: 54.9 us -> 0 us
  between operations: 14.9 us -> 0.03 us
  matrix products: 5.82 us -> 0 us
  local copies, waits for them, and re-layouts: 6.29 us -> 2.38 us
    psum x1 -> x0, waiting for transfers between devices: 123 us -> none  [shards(): gram_total = lax.psum(gram_part, ('read', 'row'))]
    pallas_call x0 -> x3, Pallas kernels: none -> 109 us  [the longest x1 52.7 us: direct(): pl.pallas_call(functools.partial(gram_kernel, count, count_row, chunks),...]
    all_to_all x2 -> x0, blocking collectives: 77.1 us -> none  [the longest x1 40.5 us: shards(): lax.all_to_all(snapshots, ('read', 'row'), split_axis=1, concat_axis=0, t...]
    another operation x9 -> x0, other arithmetic: 53.9 us -> none  [the longest x6 34 us: lower_cholesky(): return jnp.linalg.cholesky(matrix)]
    dot_general x3 -> x0, matrix products: 4.52 us -> none  [the longest x1 1.94 us: inner_products(): lax.dot_general(left_block, right_block, (((1,), (1,)), ((), ())), precis...]
    another operation x9 -> x0, local copies, waits for them, and re-layouts: 4.16 us -> none
  transfers between devices with their start and end apart: 1 -> 0, of which waited for: 1 -> 0; matrix products, arithmetic and copies ran while one was open for 0% -> 0% of each run, Pallas kernels for 0% -> 0%
where the time goes in v1:
time: 112 us
  Pallas kernels  109 us (97%)
  local copies, waits for them, and re-layouts  2.38 us (2%)
    pallas_call x1, Pallas kernels, direct(): pl.pallas_call(functools.partial(gram_kernel, count, count_row, chunks),...  52.7 us
    pallas_call x1, Pallas kernels, direct(): pl.pallas_call(functools.partial(modes_kernel, count, count_row, 4), out_...  32.6 us
    pallas_call x1, Pallas kernels, factor(): pl.pallas_call(functools.partial(factor_kernel, 64, scale), out_shape=jax...  23.9 us
    unnamed x5, local copies, waits for them, and re-layouts  2.38 us

profile of v1, /device:TPU:0, one launch (start us, length us, event | category | flops | bytes accessed | tf_op | source)
XLA Modules:
  0.0 111.6 jit_solution(14123656398967695841)
XLA Ops:
  0.0 0.0 copy-start
  0.0 1.3 %copy-done = f32[8,40960]{1,0:T(8,128)S(1)} copy-done((f32[8,40960]{1,0:T(8,128)S(1)}, f32[8,40960]{1,0:T(8,128)}, u32[]{:S(2)}) %copy-start) | copy-done | bytes 1310744
  1.3 0.0 copy-start.1
  1.3 52.7 %gram.1 = (f32[256,256]{1,0:T(8,128)S(1)}, f32[256,1280]{1,0:T(8,128)S(1)}) custom-call(f32[8,40960]{1,0:T(8,128)S(1)} %copy-done), custom_call_target="tpu_custom_call" | custom-call | flops 167772160 | bytes 2621440 | tf_op jit(solution)/shard_map/gram/pallas_call | solution.py:238
  54.0 0.0 copy-done.1
  54.0 23.9 %factor.1.fold_ref = f32[256,256]{1,0:T(8,128)S(1)} custom-call(f32[256,256]{1,0:T(8,128)S(1)} %get-tuple-element.7.gram_ref, f32[256,256]{1,0:T(8,128)S(1)} %copy-done.1), custom_call_target="tpu_custom_call" | custom-call | flops 100663296 | bytes 786432 | tf_op jit(solution)/shard_map/factor/pallas_call | solution.py:222
  78.0 32.6 %modes.1 = f32[8,40960]{1,0:T(8,128)S(1)} custom-call(f32[256,256]{1,0:T(8,128)S(1)} %factor.1.fold_ref, f32[256,1280]{1,0:T(8,128)S(1)} %get-tuple-element.8.held_ref), custom_call_target="tpu_custom_call" | custom-call | flops 167772160 | bytes 2621440 | tf_op jit(solution)/shard_map/modes/pallas_call | solution.py:260
  110.6 1.1 copy.4
Async XLA Ops:
  0.0 1.3 %copy-start = (f32[8,40960]{1,0:T(8,128)S(1)}, f32[8,40960]{1,0:T(8,128)}, u32[]{:S(2)}) copy-start(f32[8,40960]{1,0:T(8,128)} %snap_ref.1) | copy-start | bytes 3932164
  1.3 52.7 %copy-start.1 = (f32[256,256]{1,0:T(8,128)S(1)}, f32[256,256]{1,0:T(8,128)}, u32[]{:S(2)}) copy-start(f32[256,256]{1,0:T(8,128)} %coef_ref.1) | copy-start | bytes 786436

commit v2 on v1

--- a/solution.py
+++ b/solution.py
@@ -12,7 +12,8 @@
 HIGHEST = lax.Precision.HIGHEST
 NN = (((1,), (0,)), ((), ()))
 NT = (((1,), (1,)), ((), ()))
-VMEM_BYTES = 48 * 1024 * 1024
+VMEM_BYTES = 60 * 1024 * 1024
+GROUP = 16
 
 
 def product(left, right, dims=NN):
@@ -164,19 +165,23 @@
     size = block.shape[0]
     row_id = lax.broadcasted_iota(jnp.int32, (size, 2 * size), 0)
     col_id = lax.broadcasted_iota(jnp.int32, (size, 2 * size), 1)
-    state = jnp.concatenate([block, jnp.zeros_like(block)], axis=1)
-    state = jnp.where(col_id == row_id + size, 1.0, state)
-    for k in range(size - 1):
-        pivot_row = state[k : k + 1, :]
-        inverse = 1.0 / state[k : k + 1, k : k + 1]
-        scaled = pivot_row * inverse
-        low = (k + 1) // 8 * 8
-        below = state[low:, :]
-        column = below[:, k : k + 1]
-        if low <= k:
-            column = jnp.where(row_id[low:, :1] > k, column, 0.0)
-        below = below - column * scaled
-        state = jnp.concatenate([state[:low], below], axis=0) if low else below
+    active = jnp.concatenate([block, jnp.zeros_like(block)], axis=1)
+    active = jnp.where(col_id == row_id + size, 1.0, active)
+    done = []
+    for start in range(0, size, GROUP):
+        below = row_id[: size - start]
+        columns = [
+            jnp.broadcast_to(active[:, start + j : start + j + 1], active.shape) for j in range(GROUP)
+        ]
+        for j in range(GROUP):
+            inverse = 1.0 / columns[j][j : j + 1, :]
+            ratio = jnp.where(below > j, columns[j] * inverse, 0.0)
+            for i in range(j + 1, GROUP):
+                columns[i] = columns[i] - ratio * columns[i][j : j + 1, :]
+            active = active - ratio * active[j : j + 1, :]
+        done.append(active[:GROUP])
+        active = active[GROUP:]
+    state = jnp.concatenate(done, axis=0)
     pivots = jnp.sum(jnp.where(col_id == row_id, state, 0.0), axis=1, keepdims=True)
     return state[:, size:] * lax.rsqrt(pivots)
 

time: 112 us -> 102 us (0.911)
  Pallas kernels: 109 us -> 98.6 us
    pallas_call x1, Pallas kernels: 23.9 us -> 10.6 us  [factor(): pl.pallas_call(functools.partial(factor_kernel, 64, scale), out_shape=jax...]
    pallas_call x1, Pallas kernels: 52.7 us -> 54.1 us  [direct(): pl.pallas_call(functools.partial(gram_kernel, count, count_row, chunks),...]
    pallas_call x1, Pallas kernels: 32.6 us -> 33.8 us  [direct(): pl.pallas_call(functools.partial(modes_kernel, count, count_row, 4), out_...]
    unnamed x5 -> x1, local copies, waits for them, and re-layouts: 2.38 us -> 2.46 us
where the time goes in v2:
time: 102 us; the launch traced here: 101 us
  Pallas kernels  98.6 us (97%)
  local copies, waits for them, and re-layouts  2.46 us (2%)
    pallas_call x1, Pallas kernels, direct(): pl.pallas_call(functools.partial(gram_kernel, count, count_row, chunks),...  54.1 us
    pallas_call x1, Pallas kernels, direct(): pl.pallas_call(functools.partial(modes_kernel, count, count_row, 4), out_...  33.8 us
    pallas_call x1, Pallas kernels, factor(): pl.pallas_call(functools.partial(factor_kernel, 64, scale), out_shape=jax...  10.6 us
    unnamed x1, local copies, waits for them, and re-layouts  2.46 us

profile of v2, /device:TPU:0, one launch (start us, length us, event | category | flops | bytes accessed | tf_op | source)
XLA Modules:
  0.0 101.1 jit_solution(14215574489585666560)
XLA Ops:
  0.0 54.1 %gram.1 = (f32[256,256]{1,0:T(8,128)}, f32[256,1280]{1,0:T(8,128)}) custom-call(f32[8,40960]{1,0:T(8,128)} %snap_ref.1), custom_call_target="tpu_custom_call" | custom-call | flops 167772160 | bytes 2621440 | tf_op jit(solution)/shard_map/gram/pallas_call | solution.py:243
  54.1 10.6 %factor.1.fold_ref = f32[256,256]{1,0:T(8,128)} custom-call(f32[256,256]{1,0:T(8,128)} %get-tuple-element.7.gram_ref, f32[256,256]{1,0:T(8,128)} %coef_ref.1), custom_call_target="tpu_custom_call" | custom-call | flops 100663296 | bytes 786432 | tf_op jit(solution)/shard_map/factor/pallas_call | solution.py:227
  64.8 33.8 %modes.1 = f32[8,40960]{1,0:T(8,128)} custom-call(f32[256,256]{1,0:T(8,128)} %factor.1.fold_ref, f32[256,1280]{1,0:T(8,128)} %get-tuple-element.8.held_ref), custom_call_target="tpu_custom_call" | custom-call | flops 167772160 | bytes 2621440 | tf_op jit(solution)/shard_map/modes/pallas_call | solution.py:265
  98.6 2.5 %copy.4 = f32[8,40960]{1,0:T(8,128)} copy(f32[8,40960]{1,0:T(8,128)} %modes.1) | data formatting | bytes 2621440

commit v3 on v2

v3 whole, which is shorter than its diff:
```python
import functools
import math

import jax
import jax.numpy as jnp
from jax import lax
from jax.experimental import pallas as pl
from jax.experimental.pallas import tpu as pltpu
from jax.sharding import PartitionSpec as P

AXES = ("read", "row")
HIGHEST = lax.Precision.HIGHEST
NN = (((1,), (0,)), ((), ()))
NT = (((1,), (1,)), ((), ()))
VMEM_BYTES = 60 * 1024 * 1024
GROUP = 16
BLOCK = 64


def product(left, right, dims=NN):
    return lax.dot_general(left, right, dims, precision=HIGHEST, preferred_element_type=jnp.float32)


def coordinates(index, count_row):
    return (lax.div(index, count_row), lax.rem(index, count_row))


def greet(count, count_row, me):
    barrier = pltpu.get_barrier_semaphore()

    def signal(offset, carry):
        other = lax.rem(me + offset, count)
        pl.semaphore_signal(
            barrier, inc=1, device_id=coordinates(other, count_row), device_id_type=pl.DeviceIdType.MESH
        )
        return carry

    lax.fori_loop(1, count, signal, 0)
    return barrier


def wait_bytes(ref, semaphore):
    pltpu.make_async_copy(ref, ref, semaphore).wait()


def modes_kernel(count, count_row, chunks, size, scale, snap_ref, coef_ref, out_ref,
                 held, twin, part, slabs, levels, gram, work, inverse, fold, modes,
                 local_sem, send_sem, recv_sem):
    share = snap_ref.shape[0]
    snaps, width = held.shape
    piece = width // chunks
    half_row = count_row // 2
    half = count // 2
    layers = count_row // 2
    plane = count // layers
    strip = snaps // plane
    read, row = lax.axis_index("read"), lax.axis_index("row")
    me = read * count_row + row
    side = lax.div(row, half_row)
    partner = read * count_row + lax.rem(row + half_row, count_row)
    place = read * half_row + lax.rem(row, half_row)
    layer, core = lax.div(row, 2), lax.rem(row, 2)
    spot = read * 2 + core

    def rows_of(index, length):
        return pl.ds(pl.multiple_of(index * length, length), length)

    def columns_of(index):
        return pl.ds(pl.multiple_of(index * width, width), width)

    def in_half(index):
        return lax.div(index, half_row) * count_row + side * half_row + lax.rem(index, half_row)

    def mirrored(device):
        other_row = lax.rem(lax.rem(device, count_row) + half_row, count_row)
        return lax.div(device, count_row) * count_row + other_row

    def slab_of(column, which):
        start = (column * count_row + which * half_row) * share
        return pl.ds(pl.multiple_of(start, share), half_row * share)

    def send(source, target, other, stage):
        pltpu.make_async_remote_copy(
            src_ref=source,
            dst_ref=target,
            send_sem=send_sem.at[stage],
            recv_sem=recv_sem.at[stage],
            device_id=coordinates(other, count_row),
            device_id_type=pl.DeviceIdType.MESH,
        ).start()

    mine = rows_of(me, share)
    twin_stage, fetch_stage, scatter_stage, layer_stage, share_stage, out_stage = range(chunks, chunks + 6)

    barrier = greet(count, count_row, me)
    own = pltpu.make_async_copy(snap_ref.at[:, columns_of(me)], held.at[mine, :], local_sem.at[0])
    own.start()
    own_twin = pltpu.make_async_copy(snap_ref.at[:, columns_of(partner)], twin.at[mine, :], local_sem.at[1])
    own_twin.start()
    pl.semaphore_wait(barrier, count - 1)

    for chunk in range(chunks):
        def scatter(offset, carry, chunk=chunk):
            other = lax.rem(me + offset, count)
            send(
                snap_ref.at[:, pl.ds(pl.multiple_of(other * width + chunk * piece, 128), piece)],
                held.at[mine, pl.ds(chunk * piece, piece)],
                other,
                chunk,
            )
            return carry

        lax.fori_loop(1, count, scatter, 0)

    def scatter_twin(offset, carry):
        other = in_half(lax.rem(place + offset, half))
        send(snap_ref.at[:, columns_of(mirrored(other))], twin.at[mine, :], other, twin_stage)
        return carry

    lax.fori_loop(1, half, scatter_twin, 0)

    own.wait()
    for chunk in range(chunks):
        columns = pl.ds(chunk * piece, piece)
        wait_bytes(held.at[pl.ds(0, (count - 1) * share), columns], recv_sem.at[chunk])
        block = held[:, columns]
        term = product(block, block, NT)
        if chunk:
            part[...] += term
        else:
            part[...] = term

    for column in range(count // count_row):
        slab = slab_of(column, side)
        send(held.at[slab, :], twin.at[slab, :], partner, fetch_stage)

    slabs[pl.ds(spot, 1)] = part[rows_of(spot, strip), :][None]

    def at_spot(index):
        return lax.div(index, 2) * count_row + layer * 2 + lax.rem(index, 2)

    def scatter_part(offset, carry):
        index = lax.rem(spot + offset, plane)
        send(part.at[rows_of(index, strip), :], slabs.at[spot], at_spot(index), scatter_stage)
        return carry

    lax.fori_loop(1, plane, scatter_part, 0)
    wait_bytes(part.at[pl.ds(0, (plane - 1) * strip), :], recv_sem.at[scatter_stage])
    levels[pl.ds(layer, 1)] = jnp.sum(slabs[...], axis=0)[None]

    def exchange_layer(offset, carry):
        index = lax.rem(layer + offset, layers)
        send(levels.at[layer], levels.at[layer], read * count_row + index * 2 + core, layer_stage)
        return carry

    lax.fori_loop(1, layers, exchange_layer, 0)
    wait_bytes(part.at[pl.ds(0, (layers - 1) * strip), :], recv_sem.at[layer_stage])
    strip_rows = rows_of(spot, strip)
    gram[strip_rows, :] = jnp.sum(levels[...], axis=0)

    def share_total(offset, carry):
        index = lax.rem(spot + offset, plane)
        send(gram.at[strip_rows, :], gram.at[strip_rows, :], at_spot(index), share_stage)
        return carry

    lax.fori_loop(1, plane, share_total, 0)
    wait_bytes(part.at[pl.ds(0, (plane - 1) * strip), :], recv_sem.at[share_stage])

    factor_kernel(size, scale, gram, coef_ref, fold, work, inverse)
    mine_fold = jnp.concatenate(
        [fold[slab_of(column, side), :] for column in range(count // count_row)], axis=0
    )

    copies = []
    for turn, (held_ref, owner) in enumerate(((held, me), (twin, partner))):
        if turn:
            own_twin.wait()
            wait_bytes(twin.at[pl.ds(0, (half - 1) * share), :], recv_sem.at[twin_stage])
            wait_bytes(twin.at[pl.ds(0, half * share), :], recv_sem.at[fetch_stage])
        modes[turn] = product(mine_fold, held_ref[...])
        target = out_ref.at[:, columns_of(owner)]
        copy = pltpu.make_async_copy(modes.at[turn, rows_of(place, share), :], target, local_sem.at[2 + turn])
        copy.start()
        copies.append(copy)

        def scatter_modes(offset, carry, turn=turn, target=target):
            index = lax.rem(place + offset, half)
            send(modes.at[turn, rows_of(index, share), :], target, in_half(index), out_stage + turn)
            return carry

        lax.fori_loop(1, half, scatter_modes, 0)

    for copy in copies:
        copy.wait()
    half_bytes = twin.at[pl.ds(0, (half - 1) * share), :]
    for turn in range(2):
        wait_bytes(half_bytes, recv_sem.at[out_stage + turn])
        wait_bytes(half_bytes, send_sem.at[out_stage + turn])
    for chunk in range(chunks):
        wait_bytes(held.at[pl.ds(0, (count - 1) * share), pl.ds(0, piece)], send_sem.at[chunk])
    wait_bytes(half_bytes, send_sem.at[twin_stage])
    wait_bytes(twin.at[pl.ds(0, half * share), :], send_sem.at[fetch_stage])
    wait_bytes(part.at[pl.ds(0, (plane - 1) * strip), :], send_sem.at[scatter_stage])
    wait_bytes(part.at[pl.ds(0, (layers - 1) * strip), :], send_sem.at[layer_stage])
    wait_bytes(part.at[pl.ds(0, (plane - 1) * strip), :], send_sem.at[share_stage])


def eliminate(block):
    size = block.shape[0]
    row_id = lax.broadcasted_iota(jnp.int32, (size, 2 * size), 0)
    col_id = lax.broadcasted_iota(jnp.int32, (size, 2 * size), 1)
    active = jnp.concatenate([block, jnp.zeros_like(block)], axis=1)
    active = jnp.where(col_id == row_id + size, 1.0, active)
    done = []
    for start in range(0, size, GROUP):
        below = row_id[: size - start]
        columns = [
            jnp.broadcast_to(active[:, start + j : start + j + 1], active.shape) for j in range(GROUP)
        ]
        for j in range(GROUP):
            inverse = 1.0 / columns[j][j : j + 1, :]
            ratio = jnp.where(below > j, columns[j] * inverse, 0.0)
            for i in range(j + 1, GROUP):
                columns[i] = columns[i] - ratio * columns[i][j : j + 1, :]
            active = active - ratio * active[j : j + 1, :]
        done.append(active[:GROUP])
        active = active[GROUP:]
    state = jnp.concatenate(done, axis=0)
    pivots = jnp.sum(jnp.where(col_id == row_id, state, 0.0), axis=1, keepdims=True)
    return state[:, size:] * lax.rsqrt(pivots)


def factor_kernel(size, scale, gram_ref, coef_ref, fold_ref, work, inverse):
    total = gram_ref.shape[0]
    blocks = total // size
    work[...] = gram_ref[...]
    inverse[...] = jnp.zeros_like(inverse)
    for k in range(blocks):
        here = slice(k * size, (k + 1) * size)
        low = eliminate(work[here, here])
        before = slice(0, k * size)
        after = slice((k + 1) * size, total)
        if k:
            inverse[here, before] = product(low, inverse[here, before])
        inverse[here, here] = low
        if k < blocks - 1:
            across = product(low, work[here, after])
            down = product(work[after, here], low, NT)
            work[after, after] -= product(down, across)
            inverse[after, slice(0, (k + 1) * size)] -= product(down, inverse[here, slice(0, (k + 1) * size)])
    fold_ref[...] = scale * lax.dot_general(
        coef_ref[...], inverse[...], (((0,), (0,)), ((), ())),
        precision=HIGHEST, preferred_element_type=jnp.float32,
    )


def vmem_spec():
    return pl.BlockSpec(memory_space=pltpu.VMEM)


def any_spec():
    return pl.BlockSpec(memory_space=pl.ANY)


def cost(flops, moved):
    return pl.CostEstimate(flops=flops, bytes_accessed=moved, transcendentals=0)


def factor(gram, coefficients, scale):
    snaps = gram.shape[0]
    return pl.pallas_call(
        functools.partial(factor_kernel, BLOCK, scale),
        out_shape=jax.ShapeDtypeStruct((coefficients.shape[1], snaps), jnp.float32),
        in_specs=[vmem_spec()] * 2,
        out_specs=vmem_spec(),
        scratch_shapes=[pltpu.VMEM((snaps, snaps), jnp.float32)] * 2,
        compiler_params=pltpu.CompilerParams(vmem_limit_bytes=VMEM_BYTES),
        cost_estimate=cost(6 * snaps**3, 12 * snaps**2),
        name="factor",
    )(gram, coefficients)


def direct(snapshots, coefficients, count, count_row):
    share, total_rows = snapshots.shape
    snaps, width = share * count, total_rows // count
    layers = count_row // 2
    plane = count // layers
    strip = snaps // plane
    chunks = 2 if width % 256 == 0 else 1
    square = pltpu.VMEM((snaps, snaps), jnp.float32)
    return pl.pallas_call(
        functools.partial(modes_kernel, count, count_row, chunks, BLOCK, math.sqrt(total_rows)),
        out_shape=jax.ShapeDtypeStruct((share, total_rows), jnp.float32),
        in_specs=[any_spec(), vmem_spec()],
        out_specs=any_spec(),
        scratch_shapes=[
            pltpu.VMEM((snaps, width), jnp.float32),
            pltpu.VMEM((snaps, width), jnp.float32),
            square,
            pltpu.VMEM((plane, strip, snaps), jnp.float32),
            pltpu.VMEM((layers, strip, snaps), jnp.float32),
            square,
            square,
            square,
            square,
            pltpu.VMEM((2, snaps // 2, width), jnp.float32),
            pltpu.SemaphoreType.DMA((4,)),
            pltpu.SemaphoreType.DMA((chunks + 7,)),
            pltpu.SemaphoreType.DMA((chunks + 7,)),
        ],
        compiler_params=pltpu.CompilerParams(
            collective_id=0, has_side_effects=True, vmem_limit_bytes=VMEM_BYTES
        ),
        cost_estimate=cost(4 * snaps * snaps * width, 16 * snaps * width),
        name="modes",
    )(snapshots, coefficients)


def shards(snapshots, coefficients):
    count_row = lax.axis_size("row")
    count = lax.axis_size("read") * count_row
    if snapshots.shape[0] % 8 == 0 and count_row % 4 == 0:
        return direct(snapshots, coefficients, count, count_row)
    held = lax.all_to_all(snapshots, AXES, split_axis=1, concat_axis=0, tiled=True)
    gram = lax.psum(product(held, held, NT), AXES)
    folded = factor(gram, coefficients, math.sqrt(snapshots.shape[1]))
    return lax.all_to_all(product(folded, held), AXES, split_axis=0, concat_axis=1, tiled=True)


def solution(mesh):
    in_specs = (P(AXES, None), P())
    out_specs = P(AXES, None)
    return jax.shard_map(shards, mesh=mesh, in_specs=in_specs, out_specs=out_specs, check_vma=False)
```

time: 102 us -> 106 us (1.039)
  Pallas kernels: 98.6 us -> 103 us
    pallas_call x3 -> x1, Pallas kernels: 98.6 us -> 103 us  [direct(): pl.pallas_call(functools.partial(modes_kernel, count, count_row, chunks,...]
where the time goes in v3:
time: 106 us; the launch traced here: 105 us
  Pallas kernels  103 us (97%)
  local copies, waits for them, and re-layouts  2.46 us (2%)
    pallas_call x1, Pallas kernels, direct(): pl.pallas_call(functools.partial(modes_kernel, count, count_row, chunks,...  103 us
    unnamed x1, local copies, waits for them, and re-layouts  2.46 us

profile of v3, /device:TPU:0, one launch (start us, length us, event | category | flops | bytes accessed | tf_op | source)
XLA Modules:
  0.0 105.4 jit_solution(10645711714181001724)
XLA Ops:
  0.0 102.9 %modes.1 = f32[8,40960]{1,0:T(8,128)} custom-call(f32[8,40960]{1,0:T(8,128)} %snap_ref.1, f32[256,256]{1,0:T(8,128)} %coef_ref.1), custom_call_target="tpu_custom_call" | custom-call | flops 335544320 | bytes 5242880 | tf_op jit(solution)/shard_map/modes/pallas_call | solution.py:291
  102.9 2.5 %copy.4 = f32[8,40960]{1,0:T(8,128)} copy(f32[8,40960]{1,0:T(8,128)} %modes.1) | data formatting | bytes 2621440

commit v4 on v3

--- a/solution.py
+++ b/solution.py
@@ -15,6 +15,8 @@
 VMEM_BYTES = 60 * 1024 * 1024
 GROUP = 16
 BLOCK = 64
+FETCHED = 640
+FETCH = (0, 0)
 
 
 def product(left, right, dims=NN):
@@ -44,10 +46,11 @@
 
 
 def modes_kernel(count, count_row, chunks, size, scale, snap_ref, coef_ref, out_ref,
-                 held, twin, part, slabs, levels, gram, work, inverse, fold, modes,
+                 held, twin, part, slabs, levels, gram, work, inverse, fold, modes_own, modes_far, modes_twin,
                  local_sem, send_sem, recv_sem):
     share = snap_ref.shape[0]
     snaps, width = held.shape
+    fetched = twin.shape[1]
     piece = width // chunks
     half_row = count_row // 2
     half = count // 2
@@ -65,11 +68,11 @@
     def rows_of(index, length):
         return pl.ds(pl.multiple_of(index * length, length), length)
 
-    def columns_of(index):
-        return pl.ds(pl.multiple_of(index * width, width), width)
-
-    def in_half(index):
-        return lax.div(index, half_row) * count_row + side * half_row + lax.rem(index, half_row)
+    def columns_of(index, start=0, size=width):
+        return pl.ds(pl.multiple_of(index * width + start, 128), size)
+
+    def in_half(index, which):
+        return lax.div(index, half_row) * count_row + which * half_row + lax.rem(index, half_row)
 
     def mirrored(device):
         other_row = lax.rem(lax.rem(device, count_row) + half_row, count_row)
@@ -91,11 +94,12 @@
 
     mine = rows_of(me, share)
     twin_stage, fetch_stage, scatter_stage, layer_stage, share_stage, out_stage = range(chunks, chunks + 6)
+    far_stage, last_stage = out_stage + 1, out_stage + 2
 
     barrier = greet(count, count_row, me)
     own = pltpu.make_async_copy(snap_ref.at[:, columns_of(me)], held.at[mine, :], local_sem.at[0])
     own.start()
-    own_twin = pltpu.make_async_copy(snap_ref.at[:, columns_of(partner)], twin.at[mine, :], local_sem.at[1])
+    own_twin = pltpu.make_async_copy(snap_ref.at[:, columns_of(partner, 0, fetched)], twin.at[mine, :], local_sem.at[1])
     own_twin.start()
     pl.semaphore_wait(barrier, count - 1)
 
@@ -113,8 +117,8 @@
         lax.fori_loop(1, count, scatter, 0)
 
     def scatter_twin(offset, carry):
-        other = in_half(lax.rem(place + offset, half))
-        send(snap_ref.at[:, columns_of(mirrored(other))], twin.at[mine, :], other, twin_stage)
+        other = in_half(lax.rem(place + offset, half), side)
+        send(snap_ref.at[:, columns_of(mirrored(other), 0, fetched)], twin.at[mine, :], other, twin_stage)
         return carry
 
     lax.fori_loop(1, half, scatter_twin, 0)
@@ -130,9 +134,14 @@
         else:
             part[...] = term
 
-    for column in range(count // count_row):
-        slab = slab_of(column, side)
-        send(held.at[slab, :], twin.at[slab, :], partner, fetch_stage)
+    columns_left = list(range(count // count_row))
+
+    def fetch(number):
+        for column in columns_left[:number]:
+            slab = slab_of(column, side)
+            send(held.at[slab, pl.ds(0, fetched)], twin.at[slab, :], partner, fetch_stage)
+        del columns_left[:number]
+
 
     slabs[pl.ds(spot, 1)] = part[rows_of(spot, strip), :][None]
 
@@ -145,6 +154,7 @@
         return carry
 
     lax.fori_loop(1, plane, scatter_part, 0)
+    fetch(FETCH[0])
     wait_bytes(part.at[pl.ds(0, (plane - 1) * strip), :], recv_sem.at[scatter_stage])
     levels[pl.ds(layer, 1)] = jnp.sum(slabs[...], axis=0)[None]
 
@@ -154,6 +164,7 @@
         return carry
 
     lax.fori_loop(1, layers, exchange_layer, 0)
+    fetch(FETCH[1])
     wait_bytes(part.at[pl.ds(0, (layers - 1) * strip), :], recv_sem.at[layer_stage])
     strip_rows = rows_of(spot, strip)
     gram[strip_rows, :] = jnp.sum(levels[...], axis=0)
@@ -164,41 +175,53 @@
         return carry
 
     lax.fori_loop(1, plane, share_total, 0)
+    fetch(len(columns_left))
     wait_bytes(part.at[pl.ds(0, (plane - 1) * strip), :], recv_sem.at[share_stage])
 
     factor_kernel(size, scale, gram, coef_ref, fold, work, inverse)
-    mine_fold = jnp.concatenate(
-        [fold[slab_of(column, side), :] for column in range(count // count_row)], axis=0
-    )
-
-    copies = []
-    for turn, (held_ref, owner) in enumerate(((held, me), (twin, partner))):
-        if turn:
-            own_twin.wait()
-            wait_bytes(twin.at[pl.ds(0, (half - 1) * share), :], recv_sem.at[twin_stage])
-            wait_bytes(twin.at[pl.ds(0, half * share), :], recv_sem.at[fetch_stage])
-        modes[turn] = product(mine_fold, held_ref[...])
-        target = out_ref.at[:, columns_of(owner)]
-        copy = pltpu.make_async_copy(modes.at[turn, rows_of(place, share), :], target, local_sem.at[2 + turn])
-        copy.start()
-        copies.append(copy)
-
-        def scatter_modes(offset, carry, turn=turn, target=target):
+
+    def fold_of(which):
+        return jnp.concatenate(
+            [fold[slab_of(column, which), :] for column in range(count // count_row)], axis=0
+        )
+
+    def scatter_modes(modes, target, which, stage, first):
+        def step(offset, carry):
             index = lax.rem(place + offset, half)
-            send(modes.at[turn, rows_of(index, share), :], target, in_half(index), out_stage + turn)
+            send(modes.at[rows_of(index, share), :], target, in_half(index, which), stage)
             return carry
 
-        lax.fori_loop(1, half, scatter_modes, 0)
-
-    for copy in copies:
-        copy.wait()
-    half_bytes = twin.at[pl.ds(0, (half - 1) * share), :]
-    for turn in range(2):
-        wait_bytes(half_bytes, recv_sem.at[out_stage + turn])
-        wait_bytes(half_bytes, send_sem.at[out_stage + turn])
+        lax.fori_loop(first, half, step, 0)
+
+    modes_far[...] = product(fold_of(1 - side), held[:, fetched:])
+    scatter_modes(modes_far, out_ref.at[:, columns_of(me, fetched, width - fetched)], 1 - side, far_stage, 0)
+    modes_own[...] = product(fold_of(side), held[...])
+    target = out_ref.at[:, columns_of(me)]
+    keep = pltpu.make_async_copy(modes_own.at[rows_of(place, share), :], target, local_sem.at[2])
+    keep.start()
+    scatter_modes(modes_own, target, side, out_stage, 1)
+
+    own_twin.wait()
+    wait_bytes(twin.at[pl.ds(0, (half - 1) * share), :], recv_sem.at[twin_stage])
+    wait_bytes(twin.at[pl.ds(0, half * share), :], recv_sem.at[fetch_stage])
+    modes_twin[...] = product(fold_of(side), twin[...])
+    target = out_ref.at[:, columns_of(partner, 0, fetched)]
+    keep_twin = pltpu.make_async_copy(modes_twin.at[rows_of(place, share), :], target, local_sem.at[3])
+    keep_twin.start()
+    scatter_modes(modes_twin, target, side, last_stage, 1)
+
+    keep.wait()
+    keep_twin.wait()
+    for stage, moved in (
+        (far_stage, modes_far),
+        (out_stage, modes_own.at[pl.ds(0, (half - 1) * share), :]),
+        (last_stage, modes_twin.at[pl.ds(0, (half - 1) * share), :]),
+    ):
+        wait_bytes(moved, recv_sem.at[stage])
+        wait_bytes(moved, send_sem.at[stage])
     for chunk in range(chunks):
         wait_bytes(held.at[pl.ds(0, (count - 1) * share), pl.ds(0, piece)], send_sem.at[chunk])
-    wait_bytes(half_bytes, send_sem.at[twin_stage])
+    wait_bytes(twin.at[pl.ds(0, (half - 1) * share), :], send_sem.at[twin_stage])
     wait_bytes(twin.at[pl.ds(0, half * share), :], send_sem.at[fetch_stage])
     wait_bytes(part.at[pl.ds(0, (plane - 1) * strip), :], send_sem.at[scatter_stage])
     wait_bytes(part.at[pl.ds(0, (layers - 1) * strip), :], send_sem.at[layer_stage])
@@ -286,7 +309,8 @@
     layers = count_row // 2
     plane = count // layers
     strip = snaps // plane
-    chunks = 2 if width % 256 == 0 else 1
+    chunks = 2
+    fetched = width * FETCHED // 1280 // 128 * 128
     square = pltpu.VMEM((snaps, snaps), jnp.float32)
     return pl.pallas_call(
         functools.partial(modes_kernel, count, count_row, chunks, BLOCK, math.sqrt(total_rows)),
@@ -295,7 +319,7 @@
         out_specs=any_spec(),
         scratch_shapes=[
             pltpu.VMEM((snaps, width), jnp.float32),
-            pltpu.VMEM((snaps, width), jnp.float32),
+            pltpu.VMEM((snaps, fetched), jnp.float32),
             square,
             pltpu.VMEM((plane, strip, snaps), jnp.float32),
             pltpu.VMEM((layers, strip, snaps), jnp.float32),
@@ -303,10 +327,12 @@
             square,
             square,
             square,
-            pltpu.VMEM((2, snaps // 2, width), jnp.float32),
+            pltpu.VMEM((snaps // 2, width), jnp.float32),
+            pltpu.VMEM((snaps // 2, width - fetched), jnp.float32),
+            pltpu.VMEM((snaps // 2, fetched), jnp.float32),
             pltpu.SemaphoreType.DMA((4,)),
-            pltpu.SemaphoreType.DMA((chunks + 7,)),
-            pltpu.SemaphoreType.DMA((chunks + 7,)),
+            pltpu.SemaphoreType.DMA((chunks + 8,)),
+            pltpu.SemaphoreType.DMA((chunks + 8,)),
         ],
         compiler_params=pltpu.CompilerParams(
             collective_id=0, has_side_effects=True, vmem_limit_bytes=VMEM_BYTES
@@ -319,7 +345,7 @@
 def shards(snapshots, coefficients):
     count_row = lax.axis_size("row")
     count = lax.axis_size("read") * count_row
-    if snapshots.shape[0] % 8 == 0 and count_row % 4 == 0:
+    if snapshots.shape[0] % 8 == 0 and count_row % 4 == 0 and snapshots.shape[1] % (256 * count) == 0:
         return direct(snapshots, coefficients, count, count_row)
     held = lax.all_to_all(snapshots, AXES, split_axis=1, concat_axis=0, tiled=True)
     gram = lax.psum(product(held, held, NT), AXES)

time: 106 us -> 85.9 us (0.81)
  Pallas kernels: 103 us -> 83.3 us
    pallas_call x1, Pallas kernels: 103 us -> 83.3 us  [direct(): pl.pallas_call(functools.partial(modes_kernel, count, count_row, chunks,...]
where the time goes in v4:
time: 85.9 us; the launch traced here: 85.7 us
  Pallas kernels  83.3 us (97%)
  local copies, waits for them, and re-layouts  2.46 us (3%)
    pallas_call x1, Pallas kernels, direct(): pl.pallas_call(functools.partial(modes_kernel, count, count_row, chunks,...  83.3 us
    unnamed x1, local copies, waits for them, and re-layouts  2.46 us

profile of v4, /device:TPU:0, one launch (start us, length us, event | category | flops | bytes accessed | tf_op | source)
XLA Modules:
  0.0 85.7 jit_solution(17331510502574145466)
XLA Ops:
  0.0 83.3 %modes.1 = f32[8,40960]{1,0:T(8,128)} custom-call(f32[8,40960]{1,0:T(8,128)} %snap_ref.1, f32[256,256]{1,0:T(8,128)} %coef_ref.1), custom_call_target="tpu_custom_call" | custom-call | flops 335544320 | bytes 5242880 | tf_op jit(solution)/shard_map/modes/pallas_call | solution.py:315
  83.3 2.5 %copy.4 = f32[8,40960]{1,0:T(8,128)} copy(f32[8,40960]{1,0:T(8,128)} %modes.1) | data formatting | bytes 2621440

commit v5 on v4

--- a/solution.py
+++ b/solution.py
@@ -93,6 +93,7 @@
         ).start()
 
     mine = rows_of(me, share)
+    stride = next(step for step in (5, 3, 1) if math.gcd(step, count) == 1)
     twin_stage, fetch_stage, scatter_stage, layer_stage, share_stage, out_stage = range(chunks, chunks + 6)
     far_stage, last_stage = out_stage + 1, out_stage + 2
 
@@ -105,7 +106,7 @@
 
     for chunk in range(chunks):
         def scatter(offset, carry, chunk=chunk):
-            other = lax.rem(me + offset, count)
+            other = lax.rem(me + offset * stride, count)
             send(
                 snap_ref.at[:, pl.ds(pl.multiple_of(other * width + chunk * piece, 128), piece)],
                 held.at[mine, pl.ds(chunk * piece, piece)],

time: 85.9 us -> 85.6 us (level)
  no operation moved by 1% of the time
where the time goes in v5:
time: 85.6 us; the launch traced here: 85.4 us
  Pallas kernels  83 us (97%)
  local copies, waits for them, and re-layouts  2.46 us (3%)
    pallas_call x1, Pallas kernels, direct(): pl.pallas_call(functools.partial(modes_kernel, count, count_row, chunks,...  83 us
    unnamed x1, local copies, waits for them, and re-layouts  2.46 us

profile of v5, /device:TPU:0, one launch (start us, length us, event | category | flops | bytes accessed | tf_op | source)
XLA Modules:
  0.0 85.4 jit_solution(12600128602132105544)
XLA Ops:
  0.0 83.0 %modes.1 = f32[8,40960]{1,0:T(8,128)} custom-call(f32[8,40960]{1,0:T(8,128)} %snap_ref.1, f32[256,256]{1,0:T(8,128)} %coef_ref.1), custom_call_target="tpu_custom_call" | custom-call | flops 335544320 | bytes 5242880 | tf_op jit(solution)/shard_map/modes/pallas_call | solution.py:316
  83.0 2.5 %copy.4 = f32[8,40960]{1,0:T(8,128)} copy(f32[8,40960]{1,0:T(8,128)} %modes.1) | data formatting | bytes 2621440
